TPU v7x, 32 devices: a whole 2x2x4 slice. The times are simulated.
32 devices in a mesh: grp: 2 (over x), tile: 16 (over z, y, core).
Axes of the slice: x: 2, y: 2, z: 4, core: 2. Of those that a mesh axis runs over, the one named last changes fastest.
Arguments:
- queries: bfloat16 [8192, 2560], P(('grp', 'tile')), parts along dimension 0, may hold values from -150 to 150
- key_vectors: bfloat16 [8192, 2560], P(('grp', 'tile')), parts along dimension 0, may hold values from -4 to 4
- value_vectors: bfloat16 [8192, 2560], P(('grp', 'tile')), parts along dimension 0, may hold values from -6 to 6
- query_tangent: bfloat16 [8192, 2560], P(('grp', 'tile')), parts along dimension 0, may hold values from -6 to 6
- key_tangent: bfloat16 [8192, 2560], P(('grp', 'tile')), parts along dimension 0, may hold values from -6 to 6
- value_tangent: bfloat16 [8192, 2560], P(('grp', 'tile')), parts along dimension 0, may hold values from -6 to 6
- key_tiles: int32 [32, 5], P(('grp', 'tile')), parts along dimension 0, may hold values from 0 to 15, as said below
- tile_counts: int32 [32], P(('grp', 'tile')), parts along dimension 0, may hold values from 1 to 5
Outputs:
- attended: bfloat16 [8192, 2560], P(('grp', 'tile')), parts along dimension 0
- attended_tangent: bfloat16 [8192, 2560], P(('grp', 'tile')), parts along dimension 0
There are 2 independent parts, one for each index of `grp`. A program takes and returns all parts, laid end to end along the dimension named above; each array names one. Nothing has to cross between parts.
Inputs may be any that keep to these rules, and one draw needn't show every extreme that they name: `key_tiles`: row t begins with t; its first tile_counts[t] entries are distinct tiles at most 2 away from t; the later entries are tiles at most 2 away from t and carry no weight.
All inputs are finite; a program needn't handle non-finite values.
Results may differ from a plain program's by a relative error of at most 0.0048.
Values may be sent and summed in bfloat16 or wider, within the bound.
A program may use at most 128 MiB of HBM per device.

v0:
```python
import math

import jax
import jax.numpy as jnp
from jax import lax
from jax.sharding import PartitionSpec as P

HEADS = 20
D_HEAD = 128
REACH = 2
SEL = 5


def passed_along(block, axis, distance):
    devices = range(lax.axis_size(axis))
    route = [(i - distance, i) for i in devices if i - distance in devices]
    return lax.ppermute(block, axis, route)


def contract(left_part, right_part):
    return lax.dot_general(
        left_part, right_part, (((1,), (1,)), ((), ())), preferred_element_type=jnp.float32
    )


def per_device(
    queries,
    key_vectors,
    value_vectors,
    query_tangent,
    key_tangent,
    value_tangent,
    key_tiles,
    tile_counts,
):
    tile_index = lax.axis_index("tile")
    tile_rows = queries.shape[0]
    own_tile = (key_vectors, value_vectors, key_tangent, value_tangent)
    from_below = own_tile
    from_above = own_tile
    lower_list = []
    upper_list = []
    for hop_count in range(REACH):
        from_below = passed_along(
            (from_below[0], from_below[1], from_below[2], from_below[3]), "tile", 1
        )
        from_above = passed_along(
            (from_above[0], from_above[1], from_above[2], from_above[3]), "tile", -1
        )
        lower_list.append(from_below)
        upper_list.append(from_above)
    pieces = lower_list[::-1] + [own_tile] + upper_list
    key_all = jnp.concatenate([piece[0] for piece in pieces], axis=0)
    value_all = jnp.concatenate([piece[1] for piece in pieces], axis=0)
    ktan_all = jnp.concatenate([piece[2] for piece in pieces], axis=0)
    vtan_all = jnp.concatenate([piece[3] for piece in pieces], axis=0)
    live_slots = jnp.arange(SEL) < tile_counts[0]
    window_offsets = jnp.arange(-REACH, REACH + 1)
    matches = live_slots[None, :] & (key_tiles[0][None, :] == tile_index + window_offsets[:, None])
    selected = jnp.any(matches, axis=1)
    key_mask = jnp.repeat(selected, tile_rows)
    score_scale = 1.0 / math.sqrt(D_HEAD)

    def per_head(head, outputs):
        primal_out, tangent_out = outputs
        start = head * D_HEAD

        def column_cut(matrix):
            return lax.dynamic_slice_in_dim(matrix, start, D_HEAD, 1)

        query_head = column_cut(queries)
        qtan_head = column_cut(query_tangent)
        key_head = column_cut(key_all)
        ktan_head = column_cut(ktan_all)
        value_head = column_cut(value_all)
        vtan_head = column_cut(vtan_all)
        scores = contract(query_head, key_head) * score_scale
        score_tangent = (
            contract(qtan_head, key_head) + contract(query_head, ktan_head)
        ) * score_scale
        scores = jnp.where(key_mask[None, :], scores, -jnp.inf)
        row_max = jnp.max(scores, axis=1, keepdims=True)
        expo = jnp.exp(scores - row_max)
        total = jnp.sum(expo, axis=1, keepdims=True)
        shift_mean = jnp.sum(expo * score_tangent, axis=1, keepdims=True) / total
        weights_low = expo.astype(jnp.bfloat16)
        tangent_low = (expo * (score_tangent - shift_mean)).astype(jnp.bfloat16)
        primal_sum = jnp.dot(weights_low, value_head, preferred_element_type=jnp.float32)
        tangent_sum = jnp.dot(
            tangent_low, value_head, preferred_element_type=jnp.float32
        ) + jnp.dot(weights_low, vtan_head, preferred_element_type=jnp.float32)
        primal_out = lax.dynamic_update_slice_in_dim(
            primal_out, (primal_sum / total).astype(jnp.bfloat16), start, 1
        )
        tangent_out = lax.dynamic_update_slice_in_dim(
            tangent_out, (tangent_sum / total).astype(jnp.bfloat16), start, 1
        )
        return (primal_out, tangent_out)

    empty = jnp.zeros(queries.shape, jnp.bfloat16)
    attended, attended_tangent = lax.fori_loop(0, HEADS, per_head, (empty, empty))
    return (attended, attended_tangent)


def solution(mesh):
    placed = (
        P(("grp", "tile"), None),
        P(("grp", "tile"), None),
        P(("grp", "tile"), None),
        P(("grp", "tile"), None),
        P(("grp", "tile"), None),
        P(("grp", "tile"), None),
        P(("grp", "tile"), None),
        P(("grp", "tile")),
    )
    return jax.shard_map(
        per_device,
        mesh=mesh,
        in_specs=placed,
        out_specs=(P(("grp", "tile"), None), P(("grp", "tile"), None)),
        check_vma=False,
    )
```

profile of v0, /device:TPU:1, one launch (start us, length us, event | category | flops | bytes accessed | tf_op | source)
XLA Modules:
  0.0 417.7 jit_solution(8998709877481469466)
XLA Ops:
  0.6 4.5 %collective-permute-start.8 = (bf16[256,2560]{1,0:T(8,128)(2,1)}, bf16[256,2560]{1,0:T(8,128)(2,1)}, u32[]{:S(2)}, u32[]{:S(2)}) collective-permute-start(bf16[256,2560]{1,0:T(8,128)(2,1)} %param.14), channel_id=1, source_target_pairs={{0,1},{1,2},{2,3},{3,4},{4,5},{5,6},{6,7},{7,8},{8,9},{9,10},{10,1... | collective-permute-start | bytes 3932168 | tf_op jit(solution)/shard_map/ppermute | solution.py:17
  5.2 1.9 collective-permute-start.12
  7.1 12.9 %collective-permute-done.8 = bf16[256,2560]{1,0:T(8,128)(2,1)} collective-permute-done((bf16[256,2560]{1,0:T(8,128)(2,1)}, bf16[256,2560]{1,0:T(8,128)(2,1)}, u32[]{:S(2)}, u32[]{:S(2)}) %collective-permute-start.8) | collective-permute-done | bytes 1310752 | tf_op jit(solution)/shard_map/ppermute | solution.py:17
  20.0 4.4 %collective-permute-start.9 = (bf16[256,2560]{1,0:T(8,128)(2,1)}, bf16[256,2560]{1,0:T(8,128)(2,1)}, u32[]{:S(2)}, u32[]{:S(2)}) collective-permute-start(bf16[256,2560]{1,0:T(8,128)(2,1)} %collective-permute-done.8), channel_id=1, source_target_pairs={{0,1},{1,2},{2,3},{3,4},{4,5},{5,6},{6,7},{7,8},{8,9},{9,10},{10,1... | collective-permute-start | bytes 3932168 | tf_op jit(solution)/shard_map/ppermute | solution.py:17
  24.4 1.9 collective-permute-start.10
  26.3 3.6 collective-permute-start.4
  30.0 18.1 %collective-permute-done.12 = bf16[256,2560]{1,0:T(8,128)(2,1)} collective-permute-done((bf16[256,2560]{1,0:T(8,128)(2,1)}, bf16[256,2560]{1,0:T(8,128)(2,1)}, u32[]{:S(2)}, u32[]{:S(2)}) %collective-permute-start.12) | collective-permute-done | bytes 1310752 | tf_op jit(solution)/shard_map/ppermute | solution.py:17
  48.1 4.4 %collective-permute-start.13 = (bf16[256,2560]{1,0:T(8,128)(2,1)}, bf16[256,2560]{1,0:T(8,128)(2,1)}, u32[]{:S(2)}, u32[]{:S(2)}) collective-permute-start(bf16[256,2560]{1,0:T(8,128)(2,1)} %collective-permute-done.12), channel_id=1, source_target_pairs={{0,1},{1,2},{2,3},{3,4},{4,5},{5,6},{6,7},{7,8},{8,9},{9,10},{10,1... | collective-permute-start | bytes 3932168 | tf_op jit(solution)/shard_map/ppermute | solution.py:17
  52.5 1.9 collective-permute-start.14
  55.9 34.3 %collective-permute-done.9 = bf16[256,2560]{1,0:T(8,128)(2,1)} collective-permute-done((bf16[256,2560]{1,0:T(8,128)(2,1)}, bf16[256,2560]{1,0:T(8,128)(2,1)}, u32[]{:S(2)}, u32[]{:S(2)}) %collective-permute-start.9) | collective-permute-done | bytes 1310752 | tf_op jit(solution)/shard_map/ppermute | solution.py:17
  90.2 4.4 %collective-permute-start = (bf16[256,2560]{1,0:T(8,128)(2,1)}, bf16[256,2560]{1,0:T(8,128)(2,1)S(1)}, u32[]{:S(2)}, u32[]{:S(2)}) collective-permute-start(bf16[256,2560]{1,0:T(8,128)(2,1)} %param.11), channel_id=1, source_target_pairs={{0,1},{1,2},{2,3},{3,4},{4,5},{5,6},{6,7},{7,8},{8,9},{9,10},{10,1... | collective-permute-start | bytes 3932168 | tf_op jit(solution)/shard_map/ppermute | solution.py:17
  96.2 1.6 constant_dynamic-update-slice_fusion.13
  97.9 1.9 collective-permute-start.6
  99.8 18.6 %collective-permute-done.4 = bf16[256,2560]{1,0:T(8,128)(2,1)} collective-permute-done((bf16[256,2560]{1,0:T(8,128)(2,1)}, bf16[256,2560]{1,0:T(8,128)(2,1)}, u32[]{:S(2)}, u32[]{:S(2)}) %collective-permute-start.4) | collective-permute-done | bytes 1310752 | tf_op jit(solution)/shard_map/ppermute | solution.py:17
  118.4 1.9 collective-permute-start.2
  120.3 12.1 %collective-permute-done.13 = bf16[256,2560]{1,0:T(8,128)(2,1)} collective-permute-done((bf16[256,2560]{1,0:T(8,128)(2,1)}, bf16[256,2560]{1,0:T(8,128)(2,1)}, u32[]{:S(2)}, u32[]{:S(2)}) %collective-permute-start.13) | collective-permute-done | bytes 1310752 | tf_op jit(solution)/shard_map/ppermute | solution.py:17
  132.4 4.4 %collective-permute-start.5 = (bf16[256,2560]{1,0:T(8,128)(2,1)}, bf16[256,2560]{1,0:T(8,128)(2,1)S(1)}, u32[]{:S(2)}, u32[]{:S(2)}) collective-permute-start(bf16[256,2560]{1,0:T(8,128)(2,1)} %collective-permute-done.4), channel_id=1, source_target_pairs={{0,1},{1,2},{2,3},{3,4},{4,5},{5,6},{6,7},{7,8},{8,9},{9,10},{10,1... | collective-permute-start | bytes 3932168 | tf_op jit(solution)/shard_map/ppermute | solution.py:17
  139.8 6.6 %collective-permute-done = bf16[256,2560]{1,0:T(8,128)(2,1)S(1)} collective-permute-done((bf16[256,2560]{1,0:T(8,128)(2,1)}, bf16[256,2560]{1,0:T(8,128)(2,1)S(1)}, u32[]{:S(2)}, u32[]{:S(2)}) %collective-permute-start) | collective-permute-done | bytes 1310752 | tf_op jit(solution)/shard_map/ppermute | solution.py:17
  146.4 4.3 %collective-permute-start.1 = (bf16[256,2560]{1,0:T(8,128)(2,1)S(1)}, bf16[256,2560]{1,0:T(8,128)(2,1)S(1)}, u32[]{:S(2)}, u32[]{:S(2)}) collective-permute-start(bf16[256,2560]{1,0:T(8,128)(2,1)S(1)} %collective-permute-done), channel_id=1, source_target_pairs={{0,1},{1,2},{2,3},{3,4},{4,5},{5,6},{6,7},{7,8},{8,9},{9,10},{10,1... | collective-permute-start | bytes 3932168 | tf_op jit(solution)/shard_map/ppermute | solution.py:17
  150.8 1.9 collective-permute-start.11
  152.8 1.9 collective-permute-start.15
  154.7 1.9 collective-permute-start.7
  156.6 60.0 %collective-permute-done.5 = bf16[256,2560]{1,0:T(8,128)(2,1)S(1)} collective-permute-done((bf16[256,2560]{1,0:T(8,128)(2,1)}, bf16[256,2560]{1,0:T(8,128)(2,1)S(1)}, u32[]{:S(2)}, u32[]{:S(2)}) %collective-permute-start.5) | collective-permute-done | bytes 1310752 | tf_op jit(solution)/shard_map/ppermute | solution.py:17
  216.6 1.9 collective-permute-start.3
  220.2 10.4 %collective-permute-done.1 = bf16[256,2560]{1,0:T(8,128)(2,1)S(1)} collective-permute-done((bf16[256,2560]{1,0:T(8,128)(2,1)S(1)}, bf16[256,2560]{1,0:T(8,128)(2,1)S(1)}, u32[]{:S(2)}, u32[]{:S(2)}) %collective-permute-start.1) | collective-permute-done | bytes 1310752 | tf_op jit(solution)/shard_map/ppermute | solution.py:17
  231.6 4.6 %collective-permute-done.3 = bf16[256,2560]{1,0:T(8,128)(2,1)S(1)} collective-permute-done((bf16[256,2560]{1,0:T(8,128)(2,1)S(1)}, bf16[256,2560]{1,0:T(8,128)(2,1)S(1)}, u32[]{:S(2)}, u32[]{:S(2)}) %collective-permute-start.3) | collective-permute-done | bytes 1310752 | tf_op jit(solution)/shard_map/ppermute | solution.py:17
  238.0 1.9 copy-done
  239.9 176.3 %while.16 = (s32[]{:T(128)}, bf16[256,2560]{1,0:T(8,128)(2,1)S(1)}, bf16[256,2560]{1,0:T(8,128)(2,1)S(1)}, bf16[256,2560]{1,0:T(8,128)(2,1)}, bf16[1280,2560]{1,...) while((s32[]{:T(128)}, bf16[256,2560]{1,0:T(8,128)(2,1)S(1)}, ...), condition=%wide.region_5.6_spmd.clone, body=%wide.region_1.5_spmd.clone.sunk | while | flops 509050368 | bytes 14376124 | solution.py:101
  242.8 1.6 multiply_reduce_fusion.2
  251.6 1.6 multiply_reduce_fusion.2
  260.4 1.6 multiply_reduce_fusion.2
  269.2 1.6 multiply_reduce_fusion.2
  278.0 1.6 multiply_reduce_fusion.2
  286.9 1.6 multiply_reduce_fusion.2
  295.7 1.6 multiply_reduce_fusion.2
  304.5 1.6 multiply_reduce_fusion.2
  313.3 1.6 multiply_reduce_fusion.2
  322.2 1.6 multiply_reduce_fusion.2
  331.0 1.6 multiply_reduce_fusion.2
  339.8 1.6 multiply_reduce_fusion.2
  348.6 1.6 multiply_reduce_fusion.2
  357.4 1.6 multiply_reduce_fusion.2
  366.2 1.6 multiply_reduce_fusion.2
  375.0 1.6 multiply_reduce_fusion.2
  383.8 1.6 multiply_reduce_fusion.2
  392.7 1.6 multiply_reduce_fusion.2
  401.5 1.6 multiply_reduce_fusion.2
  410.3 1.6 multiply_reduce_fusion.2
  (210 shorter events, 153.8 us)
Async XLA Ops:
  0.6 19.4 %collective-permute-start.8 = (bf16[256,2560]{1,0:T(8,128)(2,1)}, bf16[256,2560]{1,0:T(8,128)(2,1)}, u32[]{:S(2)}, u32[]{:S(2)}) collective-permute-start(bf16[256,2560]{1,0:T(8,128)(2,1)} %param.14), channel_id=1, source_target_pairs={{0,1},{1,2},{2,3},{3,4},{4,5},{5,6},{6,7},{7,8},{8,9},{9,10},{10,1... | collective-permute-start | bytes 3932168 | tf_op jit(solution)/shard_map/ppermute | solution.py:17
  5.2 42.9 %collective-permute-start.12 = (bf16[256,2560]{1,0:T(8,128)(2,1)}, bf16[256,2560]{1,0:T(8,128)(2,1)}, u32[]{:S(2)}, u32[]{:S(2)}) collective-permute-start(bf16[256,2560]{1,0:T(8,128)(2,1)} %param.15), channel_id=1, source_target_pairs={{0,1},{1,2},{2,3},{3,4},{4,5},{5,6},{6,7},{7,8},{8,9},{9,10},{10,1... | collective-permute-start | bytes 3932168 | tf_op jit(solution)/shard_map/ppermute | solution.py:17
  20.0 70.2 %collective-permute-start.9 = (bf16[256,2560]{1,0:T(8,128)(2,1)}, bf16[256,2560]{1,0:T(8,128)(2,1)}, u32[]{:S(2)}, u32[]{:S(2)}) collective-permute-start(bf16[256,2560]{1,0:T(8,128)(2,1)} %collective-permute-done.8), channel_id=1, source_target_pairs={{0,1},{1,2},{2,3},{3,4},{4,5},{5,6},{6,7},{7,8},{8,9},{9,10},{10,1... | collective-permute-start | bytes 3932168 | tf_op jit(solution)/shard_map/ppermute | solution.py:17
  24.4 73.3 %collective-permute-start.10 = (bf16[256,2560]{1,0:T(8,128)(2,1)}, bf16[256,2560]{1,0:T(8,128)(2,1)S(1)}, u32[]{:S(2)}, u32[]{:S(2)}) collective-permute-start(bf16[256,2560]{1,0:T(8,128)(2,1)} %param.14), channel_id=1, source_target_pairs={{1,0},{2,1},{3,2},{4,3},{5,4},{6,5},{7,6},{8,7},{9,8},{10,9},{11,1... | collective-permute-start | bytes 3932168 | tf_op jit(solution)/shard_map/ppermute | solution.py:17
  26.3 92.0 %collective-permute-start.4 = (bf16[256,2560]{1,0:T(8,128)(2,1)}, bf16[256,2560]{1,0:T(8,128)(2,1)}, u32[]{:S(2)}, u32[]{:S(2)}) collective-permute-start(bf16[256,2560]{1,0:T(8,128)(2,1)} %param.12), channel_id=1, source_target_pairs={{0,1},{1,2},{2,3},{3,4},{4,5},{5,6},{6,7},{7,8},{8,9},{9,10},{10,1... | collective-permute-start | bytes 3932168 | tf_op jit(solution)/shard_map/ppermute | solution.py:17
  48.1 84.3 %collective-permute-start.13 = (bf16[256,2560]{1,0:T(8,128)(2,1)}, bf16[256,2560]{1,0:T(8,128)(2,1)}, u32[]{:S(2)}, u32[]{:S(2)}) collective-permute-start(bf16[256,2560]{1,0:T(8,128)(2,1)} %collective-permute-done.12), channel_id=1, source_target_pairs={{0,1},{1,2},{2,3},{3,4},{4,5},{5,6},{6,7},{7,8},{8,9},{9,10},{10,1... | collective-permute-start | bytes 3932168 | tf_op jit(solution)/shard_map/ppermute | solution.py:17
  52.5 98.3 %collective-permute-start.14 = (bf16[256,2560]{1,0:T(8,128)(2,1)}, bf16[256,2560]{1,0:T(8,128)(2,1)S(1)}, u32[]{:S(2)}, u32[]{:S(2)}) collective-permute-start(bf16[256,2560]{1,0:T(8,128)(2,1)} %param.15), channel_id=1, source_target_pairs={{1,0},{2,1},{3,2},{4,3},{5,4},{6,5},{7,6},{8,7},{9,8},{10,9},{11,1... | collective-permute-start | bytes 3932168 | tf_op jit(solution)/shard_map/ppermute | solution.py:17
  90.2 56.2 %collective-permute-start = (bf16[256,2560]{1,0:T(8,128)(2,1)}, bf16[256,2560]{1,0:T(8,128)(2,1)S(1)}, u32[]{:S(2)}, u32[]{:S(2)}) collective-permute-start(bf16[256,2560]{1,0:T(8,128)(2,1)} %param.11), channel_id=1, source_target_pairs={{0,1},{1,2},{2,3},{3,4},{4,5},{5,6},{6,7},{7,8},{8,9},{9,10},{10,1... | collective-permute-start | bytes 3932168 | tf_op jit(solution)/shard_map/ppermute | solution.py:17
  94.6 23.7 %copy-start.7 = (bf16[256,2560]{1,0:T(8,128)(2,1)S(1)}, bf16[256,2560]{1,0:T(8,128)(2,1)}, u32[]{:S(2)}) copy-start(bf16[256,2560]{1,0:T(8,128)(2,1)} %param.11) | copy-start | bytes 3932164
  96.2 1.7 copy-start.6
  96.2 40.6 %copy-start.4 = (bf16[256,2560]{1,0:T(8,128)(2,1)S(1)}, bf16[256,2560]{1,0:T(8,128)(2,1)}, u32[]{:S(2)}) copy-start(bf16[256,2560]{1,0:T(8,128)(2,1)} %param.14) | copy-start | bytes 3932164
  97.9 54.9 %collective-permute-start.6 = (bf16[256,2560]{1,0:T(8,128)(2,1)S(1)}, bf16[256,2560]{1,0:T(8,128)(2,1)S(1)}, u32[]{:S(2)}, u32[]{:S(2)}) collective-permute-start(bf16[256,2560]{1,0:T(8,128)(2,1)S(1)} %copy-done.6), channel_id=1, source_target_pairs={{1,0},{2,1},{3,2},{4,3},{5,4},{6,5},{7,6},{8,7},{9,8},{10,9},{11,1... | collective-permute-start | bytes 3932168 | tf_op jit(solution)/shard_map/ppermute | solution.py:17
  118.4 36.3 %collective-permute-start.2 = (bf16[256,2560]{1,0:T(8,128)(2,1)S(1)}, bf16[256,2560]{1,0:T(8,128)(2,1)S(1)}, u32[]{:S(2)}, u32[]{:S(2)}) collective-permute-start(bf16[256,2560]{1,0:T(8,128)(2,1)S(1)} %copy-done.7), channel_id=1, source_target_pairs={{1,0},{2,1},{3,2},{4,3},{5,4},{6,5},{7,6},{8,7},{9,8},{10,9},{11,1... | collective-permute-start | bytes 3932168 | tf_op jit(solution)/shard_map/ppermute | solution.py:17
  132.4 84.3 %collective-permute-start.5 = (bf16[256,2560]{1,0:T(8,128)(2,1)}, bf16[256,2560]{1,0:T(8,128)(2,1)S(1)}, u32[]{:S(2)}, u32[]{:S(2)}) collective-permute-start(bf16[256,2560]{1,0:T(8,128)(2,1)} %collective-permute-done.4), channel_id=1, source_target_pairs={{0,1},{1,2},{2,3},{3,4},{4,5},{5,6},{6,7},{7,8},{8,9},{9,10},{10,1... | collective-permute-start | bytes 3932168 | tf_op jit(solution)/shard_map/ppermute | solution.py:17
  138.3 12.4 %copy-start.5 = (bf16[256,2560]{1,0:T(8,128)(2,1)S(1)}, bf16[256,2560]{1,0:T(8,128)(2,1)}, u32[]{:S(2)}) copy-start(bf16[256,2560]{1,0:T(8,128)(2,1)} %param.15) | copy-start | bytes 3932164
  146.4 84.2 %collective-permute-start.1 = (bf16[256,2560]{1,0:T(8,128)(2,1)S(1)}, bf16[256,2560]{1,0:T(8,128)(2,1)S(1)}, u32[]{:S(2)}, u32[]{:S(2)}) collective-permute-start(bf16[256,2560]{1,0:T(8,128)(2,1)S(1)} %collective-permute-done), channel_id=1, source_target_pairs={{0,1},{1,2},{2,3},{3,4},{4,5},{5,6},{6,7},{7,8},{8,9},{9,10},{10,1... | collective-permute-start | bytes 3932168 | tf_op jit(solution)/shard_map/ppermute | solution.py:17
  150.8 80.4 %collective-permute-start.11 = (bf16[256,2560]{1,0:T(8,128)(2,1)S(1)}, bf16[256,2560]{1,0:T(8,128)(2,1)S(1)}, u32[]{:S(2)}, u32[]{:S(2)}) collective-permute-start(bf16[256,2560]{1,0:T(8,128)(2,1)S(1)} %collective-permute-done.10), channel_id=1, source_target_pairs={{1,0},{2,1},{3,2},{4,3},{5,4},{6,5},{7,6},{8,7},{9,8},{10,9},{11,1... | collective-permute-start | bytes 3932168 | tf_op jit(solution)/shard_map/ppermute | solution.py:17
  152.8 78.6 %collective-permute-start.15 = (bf16[256,2560]{1,0:T(8,128)(2,1)S(1)}, bf16[256,2560]{1,0:T(8,128)(2,1)S(1)}, u32[]{:S(2)}, u32[]{:S(2)}) collective-permute-start(bf16[256,2560]{1,0:T(8,128)(2,1)S(1)} %collective-permute-done.14), channel_id=1, source_target_pairs={{1,0},{2,1},{3,2},{4,3},{5,4},{6,5},{7,6},{8,7},{9,8},{10,9},{11,1... | collective-permute-start | bytes 3932168 | tf_op jit(solution)/shard_map/ppermute | solution.py:17
  154.7 76.8 %collective-permute-start.7 = (bf16[256,2560]{1,0:T(8,128)(2,1)S(1)}, bf16[256,2560]{1,0:T(8,128)(2,1)S(1)}, u32[]{:S(2)}, u32[]{:S(2)}) collective-permute-start(bf16[256,2560]{1,0:T(8,128)(2,1)S(1)} %collective-permute-done.6), channel_id=1, source_target_pairs={{1,0},{2,1},{3,2},{4,3},{5,4},{6,5},{7,6},{8,7},{9,8},{10,9},{11,1... | collective-permute-start | bytes 3932168 | tf_op jit(solution)/shard_map/ppermute | solution.py:17
  216.6 19.6 %collective-permute-start.3 = (bf16[256,2560]{1,0:T(8,128)(2,1)S(1)}, bf16[256,2560]{1,0:T(8,128)(2,1)S(1)}, u32[]{:S(2)}, u32[]{:S(2)}) collective-permute-start(bf16[256,2560]{1,0:T(8,128)(2,1)S(1)} %collective-permute-done.2), channel_id=1, source_target_pairs={{1,0},{2,1},{3,2},{4,3},{5,4},{6,5},{7,6},{8,7},{9,8},{10,9},{11,1... | collective-permute-start | bytes 3932168 | tf_op jit(solution)/shard_map/ppermute | solution.py:17
  231.3 4.9 %copy-start.1 = (bf16[1280,2560]{1,0:T(8,128)(2,1)}, bf16[1280,2560]{1,0:T(8,128)(2,1)S(1)}, u32[]{:S(2)}) copy-start(bf16[1280,2560]{1,0:T(8,128)(2,1)S(1)} %constant_dynamic-update-slice_fusion.10) | copy-start | bytes 19660804
  231.5 5.0 %copy-start.3 = (bf16[1280,2560]{1,0:T(8,128)(2,1)}, bf16[1280,2560]{1,0:T(8,128)(2,1)S(1)}, u32[]{:S(2)}) copy-start(bf16[1280,2560]{1,0:T(8,128)(2,1)S(1)} %constant_dynamic-update-slice_fusion.15) | copy-start | bytes 19660804
  231.6 6.4 %copy-start.2 = (bf16[1280,2560]{1,0:T(8,128)(2,1)}, bf16[1280,2560]{1,0:T(8,128)(2,1)S(1)}, u32[]{:S(2)}) copy-start(bf16[1280,2560]{1,0:T(8,128)(2,1)S(1)} %constant_dynamic-update-slice_fusion.5) | copy-start | bytes 19660804
  236.3 3.6 copy-start
  416.2 1.1 copy-start.8
  416.2 1.5 copy-start.9
where the time goes:
time: 422 us; the launch traced here: 418 us
  waiting for transfers between devices  178 us (42%)
  matrix products  174 us (41%)
  starting transfers between devices  47.2 us (11%)
  local copies, waits for them, and re-layouts  15.6 us (4%)
    ppermute x16, waiting for transfers between devices, passed_along(): return lax.ppermute(block, axis, route)  178 us
    dot_general x60, matrix products, contract(): lax.dot_general(left_part, right_part, (((1,), (1,)), ((), ())), preferre...  88.6 us
    ppermute x16, starting transfers between devices, passed_along(): return lax.ppermute(block, axis, route)  47.2 us
    dot_general x20, matrix products, per_head(): jnp.dot(tangent_low, value_head, preferred_element_type=jnp.float32)  28.5 us
    dot_general x20, matrix products, per_head(): jnp.dot(weights_low, vtan_head, preferred_element_type=jnp.float32)  28.2 us
    dot_general x20, matrix products, per_head(): jnp.dot(weights_low, value_head, preferred_element_type=jnp.float32)  28.2 us
    unnamed x36, local copies, waits for them, and re-layouts  13.4 us
  transfers between devices with their start and end apart: 16, of which 9 were waited for; matrix products, arithmetic and copies ran while one was open for 2% of the time, Pallas kernels for 0%

commit v1 on v0

v1 whole, which is shorter than its diff:
```python
import functools
import math

import jax
import jax.numpy as jnp
from jax import lax
from jax.experimental import pallas as pl
from jax.experimental.pallas import tpu as pltpu
from jax.sharding import PartitionSpec as P

D = 128
OWN, PAIR, NEAR, FAR, CROSS = range(5)
AHEAD = 3


def kernel(
    tiles,
    q_ref,
    k_ref,
    v_ref,
    qt_ref,
    kt_ref,
    vt_ref,
    list_ref,
    count_ref,
    out_ref,
    tan_ref,
    kv,
    qq,
    res,
    load_sem,
    q_sem,
    near_send,
    near_recv,
    pair_send,
    pair_recv,
    far_send,
    far_recv,
    cross_send,
    cross_recv,
    out_sem,
):
    heads = kv.shape[1]
    slots = list_ref.shape[1]
    me = lax.axis_index("tile")
    core = me % 2
    side = (me // 2) % 2
    pair = me + 1 - 2 * core
    near = me + 2 - 4 * side
    far_to = (me + 4 - 8 * side + tiles) % tiles
    far_from = (me - 4 + 8 * side + tiles) % tiles
    lacking = NEAR + (side + core) % 2

    def columns(h):
        return pl.ds(pl.multiple_of(h * D, D), D)

    def load(h, _):
        for a, ref in enumerate((k_ref, kt_ref, v_ref, vt_ref)):
            pltpu.make_async_copy(
                ref.at[:, columns(h)], kv.at[OWN, h, :, pl.ds(a * D, D)], load_sem.at[h]
            ).start()
        for a, ref in enumerate((qt_ref, q_ref)):
            pltpu.make_async_copy(
                ref.at[:, columns(h)], qq.at[h, :, pl.ds(a * D, D)], q_sem.at[h]
            ).start()
        return 0

    lax.fori_loop(0, heads, load, 0)

    barrier = pltpu.get_barrier_semaphore()
    for other in (pair, near, far_to, far_from):
        pl.semaphore_signal(
            barrier, inc=1, device_id={"tile": other}, device_id_type=pl.DeviceIdType.MESH
        )
    pl.semaphore_wait(barrier, 4)

    def send(source, target, h, send_sem, recv_sem, other):
        return pltpu.make_async_remote_copy(
            src_ref=kv.at[source, h],
            dst_ref=kv.at[target, h],
            send_sem=send_sem.at[h],
            recv_sem=recv_sem.at[h],
            device_id={"tile": other},
            device_id_type=pl.DeviceIdType.MESH,
        )

    def to_near(h):
        return send(OWN, NEAR, h, near_send, near_recv, near)

    def to_pair(h):
        return send(OWN, PAIR, h, pair_send, pair_recv, pair)

    def to_far(h):
        return send(NEAR, FAR, h, far_send, far_recv, far_to)

    def to_cross(h):
        return send(lacking, CROSS, h, cross_send, cross_recv, pair)

    def out_copies(h):
        return [
            pltpu.make_async_copy(res.at[i, h], ref.at[:, columns(h)], out_sem.at[i, h])
            for i, ref in enumerate((out_ref, tan_ref))
        ]

    def first(h):
        pltpu.make_async_copy(kv.at[OWN, h], kv.at[OWN, h], load_sem.at[h]).wait()
        to_near(h).start()
        to_pair(h).start()

    for h in range(AHEAD):
        first(h)

    offsets = (0, 1 - 2 * core, 2 - 4 * side, 4 * side - 2, 2 * core - 1)
    biases = []
    for offset in offsets:
        chosen = jnp.int32(0)
        for slot in range(slots):
            hit = (list_ref[0, slot] == me + offset) & (slot < count_ref[0])
            chosen = jnp.where(hit, jnp.int32(1), chosen)
        biases.append(jnp.where(chosen == 1, jnp.float32(0), jnp.float32(-jnp.inf)))

    scale = 1.0 / math.sqrt(D)
    contract = functools.partial(
        lax.dot_general,
        dimension_numbers=(((1,), (1,)), ((), ())),
        preferred_element_type=jnp.float32,
    )

    def attend(h):
        both = qq[h]
        query = both[:, D:]
        scores = [
            contract(query, kv[j, h, :, 0:D]) * scale + biases[j] for j in range(5)
        ]
        tangents = [contract(both, kv[j, h, :, 0 : 2 * D]) * scale for j in range(5)]
        row_max = functools.reduce(jnp.maximum, scores).max(axis=1, keepdims=True)
        expos = [jnp.exp(s - row_max) for s in scores]
        total = functools.reduce(jnp.add, expos).sum(axis=1, keepdims=True)
        weighted = [e * t for e, t in zip(expos, tangents)]
        inverse = 1.0 / total
        mean = functools.reduce(jnp.add, weighted).sum(axis=1, keepdims=True) * inverse
        sums = jnp.zeros((both.shape[0], 2 * D), jnp.float32)
        shifted = jnp.zeros((both.shape[0], D), jnp.float32)
        for j in range(5):
            weights_low = expos[j].astype(jnp.bfloat16)
            tangent_low = (expos[j] * (tangents[j] - mean)).astype(jnp.bfloat16)
            sums += jnp.dot(
                weights_low, kv[j, h, :, 2 * D : 4 * D], preferred_element_type=jnp.float32
            )
            shifted += jnp.dot(
                tangent_low, kv[j, h, :, 2 * D : 3 * D], preferred_element_type=jnp.float32
            )
        res[0, h] = (sums[:, :D] * inverse).astype(res.dtype)
        res[1, h] = ((shifted + sums[:, D:]) * inverse).astype(res.dtype)

    def step(g, _):
        @pl.when(g < heads)
        def _():
            to_near(g).wait_recv()
            to_far(g).start()

        @pl.when(g + AHEAD < heads)
        def _():
            first(g + AHEAD)

        @pl.when(g >= 2)
        def _():
            h = g - 2
            pltpu.make_async_copy(qq.at[h], qq.at[h], q_sem.at[h]).wait()
            to_pair(h).wait_recv()
            to_cross(h).wait_recv()
            attend(h)
            for copy in out_copies(h):
                copy.start()

        @pl.when((g >= 1) & (g < heads + 1))
        def _():
            to_far(g - 1).wait_recv()
            to_cross(g - 1).start()

        return 0

    lax.fori_loop(0, heads + 2, step, 0)

    def finish(h, _):
        to_near(h).wait_send()
        to_pair(h).wait_send()
        to_far(h).wait_send()
        to_cross(h).wait_send()
        for copy in out_copies(h):
            copy.wait()
        return 0

    lax.fori_loop(0, heads, finish, 0)


def per_device(tiles, *arrays):
    queries = arrays[0]
    rows, width = queries.shape
    heads = width // D
    shape = jax.ShapeDtypeStruct(queries.shape, queries.dtype)
    anywhere = pl.BlockSpec(memory_space=pl.ANY)
    scalars = pl.BlockSpec(memory_space=pltpu.SMEM)
    per_head = pltpu.SemaphoreType.DMA((heads,))
    return pl.pallas_call(
        functools.partial(kernel, tiles),
        out_shape=(shape, shape),
        in_specs=[anywhere] * 6 + [scalars] * 2,
        out_specs=(anywhere, anywhere),
        scratch_shapes=[
            pltpu.VMEM((5, heads, rows, 4 * D), queries.dtype),
            pltpu.VMEM((heads, rows, 2 * D), queries.dtype),
            pltpu.VMEM((2, heads, rows, D), queries.dtype),
        ]
        + [per_head] * 10
        + [pltpu.SemaphoreType.DMA((2, heads))],
        compiler_params=pltpu.CompilerParams(
            collective_id=0, has_side_effects=True, vmem_limit_bytes=56 * 1024 * 1024
        ),
        cost_estimate=pl.CostEstimate(
            flops=2 * 6 * rows * rows * 5 * width,
            bytes_accessed=16 * rows * width,
            transcendentals=5 * rows * rows * heads,
        ),
    )(*arrays)


def solution(mesh):
    placed = (P(("grp", "tile"), None),) * 7 + (P(("grp", "tile")),)
    return jax.shard_map(
        functools.partial(per_device, mesh.shape["tile"]),
        mesh=mesh,
        in_specs=placed,
        out_specs=(P(("grp", "tile"), None), P(("grp", "tile"), None)),
        check_vma=False,
    )
```

time: 422 us -> 137 us (0.32); the launches traced: 418 us -> 137 us
  waiting for transfers between devices: 178 us -> 0 us
  matrix products: 174 us -> 0 us
  Pallas kernels: 0 us -> 132 us
  starting transfers between devices: 47.2 us -> 0 us
  local copies, waits for them, and re-layouts: 15.6 us -> 3.62 us
    ppermute x16 -> x0, waiting for transfers between devices: 178 us -> none  [passed_along(): return lax.ppermute(block, axis, route)]
    dot_general x120 -> x0, matrix products: 174 us -> none  [the longest x60 88.6 us: contract(): lax.dot_general(left_part, right_part, (((1,), (1,)), ((), ())), preferre...]
    pallas_call x0 -> x1, Pallas kernels: none -> 132 us  [per_device(): pl.pallas_call(functools.partial(kernel, tiles), out_shape=(shape, shape)...]
    ppermute x16 -> x0, starting transfers between devices: 47.2 us -> none  [passed_along(): return lax.ppermute(block, axis, route)]
    unnamed x36 -> x4, local copies, waits for them, and re-layouts: 13.4 us -> 3.62 us
  transfers between devices with their start and end apart: 16 -> 0, of which waited for: 9 -> 0; matrix products, arithmetic and copies ran while one was open for 2% -> 0% of each run, Pallas kernels for 0% -> 0%
where the time goes in v1:
time: 137 us
  Pallas kernels  132 us (96%)
  local copies, waits for them, and re-layouts  3.62 us (3%)
    pallas_call x1, Pallas kernels, per_device(): pl.pallas_call(functools.partial(kernel, tiles), out_shape=(shape, shape)...  132 us
    unnamed x4, local copies, waits for them, and re-layouts  3.62 us

profile of v1, /device:TPU:1, one launch (start us, length us, event | category | flops | bytes accessed | tf_op | source)
XLA Modules:
  0.0 137.2 jit_solution(793036760867729676)
XLA Ops:
  1.3 132.3 %shard_map.95 = (bf16[256,2560]{1,0:T(8,128)(2,1)}, bf16[256,2560]{1,0:T(8,128)(2,1)}) custom-call(bf16[256,2560]{1,0:T(8,128)(2,1)} %q_ref.1, bf16[256,2560]{1,0:T(8,128)(2,1)} %k_ref.1, bf16[256,2560]{1,0:T(8,128)(2,1)} %v_ref.1, bf16[256,2560]{1,0:T(8,128)(2,1)} %qt_ref.1, bf16[256,2560]{1,0:T(8,128)(2,1)} %kt_ref.1, bf16[256,2560]{1,0:T(8,128)(2,1)} %vt_ref.1, ...), custom_call_target="tpu_custom_call" | custom-call | flops 10066329600 | bytes 10485760 | tf_op jit(solution)/shard_map/pallas_call | solution.py:205
  133.6 0.0 copy-start
  133.6 2.6 %copy.13 = bf16[256,2560]{1,0:T(8,128)(2,1)} copy(bf16[256,2560]{1,0:T(8,128)(2,1)} %get-tuple-element.4) | data formatting | bytes 2621440
  136.2 0.0 copy-done
  136.2 1.1 copy.14
Async XLA Ops:
  133.6 2.6 %copy-start = (bf16[256,2560]{1,0:T(8,128)(2,1)S(1)}, bf16[256,2560]{1,0:T(8,128)(2,1)}, u32[]{:S(2)}) copy-start(bf16[256,2560]{1,0:T(8,128)(2,1)} %get-tuple-element.5) | copy-start | bytes 3932164

commit v2 on v1

--- a/solution.py
+++ b/solution.py
@@ -10,7 +10,10 @@
 
 D = 128
 OWN, PAIR, NEAR, FAR, CROSS = range(5)
-AHEAD = 3
+PIECES = 2
+AHEAD = 4
+LAG = 2
+UNITS = 2
 
 
 def kernel(
@@ -27,7 +30,6 @@
     tan_ref,
     kv,
     qq,
-    res,
     load_sem,
     q_sem,
     near_send,
@@ -38,10 +40,13 @@
     far_recv,
     cross_send,
     cross_recv,
-    out_sem,
 ):
     heads = kv.shape[1]
     slots = list_ref.shape[1]
+    rows = kv.shape[2]
+    part = rows // PIECES
+    block = rows // UNITS
+    pieces = heads * PIECES
     me = lax.axis_index("tile")
     core = me % 2
     side = (me // 2) % 2
@@ -54,7 +59,7 @@
     def columns(h):
         return pl.ds(pl.multiple_of(h * D, D), D)
 
-    def load(h, _):
+    def load(h):
         for a, ref in enumerate((k_ref, kt_ref, v_ref, vt_ref)):
             pltpu.make_async_copy(
                 ref.at[:, columns(h)], kv.at[OWN, h, :, pl.ds(a * D, D)], load_sem.at[h]
@@ -63,52 +68,59 @@
             pltpu.make_async_copy(
                 ref.at[:, columns(h)], qq.at[h, :, pl.ds(a * D, D)], q_sem.at[h]
             ).start()
-        return 0
-
-    lax.fori_loop(0, heads, load, 0)
 
     barrier = pltpu.get_barrier_semaphore()
     for other in (pair, near, far_to, far_from):
         pl.semaphore_signal(
             barrier, inc=1, device_id={"tile": other}, device_id_type=pl.DeviceIdType.MESH
         )
+    load(0)
+    load(1)
+    load(2)
     pl.semaphore_wait(barrier, 4)
 
-    def send(source, target, h, send_sem, recv_sem, other):
+    def send(source, target, where, send_sem, recv_sem, other):
         return pltpu.make_async_remote_copy(
-            src_ref=kv.at[source, h],
-            dst_ref=kv.at[target, h],
-            send_sem=send_sem.at[h],
-            recv_sem=recv_sem.at[h],
+            src_ref=kv.at[(source, *where)],
+            dst_ref=kv.at[(target, *where)],
+            send_sem=send_sem,
+            recv_sem=recv_sem,
             device_id={"tile": other},
             device_id_type=pl.DeviceIdType.MESH,
         )
 
-    def to_near(h):
-        return send(OWN, NEAR, h, near_send, near_recv, near)
+    def piece(i):
+        return i // PIECES, pl.ds(pl.multiple_of(i % PIECES * part, part), part)
+
+    def to_near(i):
+        return send(OWN, NEAR, piece(i), near_send.at[i], near_recv.at[i], near)
 
     def to_pair(h):
-        return send(OWN, PAIR, h, pair_send, pair_recv, pair)
-
-    def to_far(h):
-        return send(NEAR, FAR, h, far_send, far_recv, far_to)
-
-    def to_cross(h):
-        return send(lacking, CROSS, h, cross_send, cross_recv, pair)
-
-    def out_copies(h):
-        return [
-            pltpu.make_async_copy(res.at[i, h], ref.at[:, columns(h)], out_sem.at[i, h])
-            for i, ref in enumerate((out_ref, tan_ref))
-        ]
-
-    def first(h):
-        pltpu.make_async_copy(kv.at[OWN, h], kv.at[OWN, h], load_sem.at[h]).wait()
-        to_near(h).start()
-        to_pair(h).start()
-
-    for h in range(AHEAD):
-        first(h)
+        return send(OWN, PAIR, (h,), pair_send.at[h], pair_recv.at[h], pair)
+
+    def to_far(i):
+        return send(NEAR, FAR, piece(i), far_send.at[i], far_recv.at[i], far_to)
+
+    def to_cross(i):
+        return send(lacking, CROSS, piece(i), cross_send.at[i], cross_recv.at[i], pair)
+
+    def first(i):
+        @pl.when(i % PIECES == 0)
+        def _():
+            h = i // PIECES
+            pltpu.make_async_copy(kv.at[OWN, h], kv.at[OWN, h], load_sem.at[h]).wait()
+
+        to_near(i).start()
+
+        @pl.when(i % PIECES == 0)
+        def _():
+            to_pair(i // PIECES).start()
+
+    def begin(i, _):
+        first(i)
+        return 0
+
+    lax.fori_loop(0, AHEAD, begin, 0)
 
     offsets = (0, 1 - 2 * core, 2 - 4 * side, 4 * side - 2, 2 * core - 1)
     biases = []
@@ -126,8 +138,9 @@
         preferred_element_type=jnp.float32,
     )
 
-    def attend(h):
-        both = qq[h]
+    def attend(h, u):
+        here = pl.ds(pl.multiple_of(u * block, block), block)
+        both = qq[h, here, :]
         query = both[:, D:]
         scores = [
             contract(query, kv[j, h, :, 0:D]) * scale + biases[j] for j in range(5)
@@ -150,45 +163,54 @@
             shifted += jnp.dot(
                 tangent_low, kv[j, h, :, 2 * D : 3 * D], preferred_element_type=jnp.float32
             )
-        res[0, h] = (sums[:, :D] * inverse).astype(res.dtype)
-        res[1, h] = ((shifted + sums[:, D:]) * inverse).astype(res.dtype)
+        out_ref[here, columns(h)] = (sums[:, :D] * inverse).astype(out_ref.dtype)
+        tan_ref[here, columns(h)] = ((shifted + sums[:, D:]) * inverse).astype(out_ref.dtype)
 
     def step(g, _):
-        @pl.when(g < heads)
+        @pl.when(g < pieces)
         def _():
             to_near(g).wait_recv()
             to_far(g).start()
 
-        @pl.when(g + AHEAD < heads)
+        @pl.when(g + AHEAD < pieces)
         def _():
             first(g + AHEAD)
 
-        @pl.when(g >= 2)
-        def _():
-            h = g - 2
-            pltpu.make_async_copy(qq.at[h], qq.at[h], q_sem.at[h]).wait()
-            to_pair(h).wait_recv()
-            to_cross(h).wait_recv()
-            attend(h)
-            for copy in out_copies(h):
-                copy.start()
-
-        @pl.when((g >= 1) & (g < heads + 1))
-        def _():
-            to_far(g - 1).wait_recv()
-            to_cross(g - 1).start()
+        @pl.when((g % PIECES == 1) & (g // PIECES + 3 < heads))
+        def _():
+            load(g // PIECES + 3)
+
+        behind = g - (PIECES + LAG)
+
+        @pl.when((behind >= 0) & (behind % (PIECES // UNITS) == 0))
+        def _():
+            h = behind // PIECES
+            u = behind % PIECES // (PIECES // UNITS)
+
+            @pl.when(u == 0)
+            def _():
+                pltpu.make_async_copy(qq.at[h], qq.at[h], q_sem.at[h]).wait()
+                to_pair(h).wait_recv()
+                for p in range(PIECES):
+                    to_cross(h * PIECES + p).wait_recv()
+
+            attend(h, u)
+
+        @pl.when((g >= LAG) & (g < pieces + LAG))
+        def _():
+            to_far(g - LAG).wait_recv()
+            to_cross(g - LAG).start()
 
         return 0
 
-    lax.fori_loop(0, heads + 2, step, 0)
+    lax.fori_loop(0, pieces + PIECES + LAG, step, 0)
 
     def finish(h, _):
-        to_near(h).wait_send()
+        for p in range(PIECES):
+            to_near(h * PIECES + p).wait_send()
+            to_far(h * PIECES + p).wait_send()
+            to_cross(h * PIECES + p).wait_send()
         to_pair(h).wait_send()
-        to_far(h).wait_send()
-        to_cross(h).wait_send()
-        for copy in out_copies(h):
-            copy.wait()
         return 0
 
     lax.fori_loop(0, heads, finish, 0)
@@ -202,18 +224,23 @@
     anywhere = pl.BlockSpec(memory_space=pl.ANY)
     scalars = pl.BlockSpec(memory_space=pltpu.SMEM)
     per_head = pltpu.SemaphoreType.DMA((heads,))
+    per_piece = pltpu.SemaphoreType.DMA((heads * PIECES,))
+    kept = pltpu.VMEM(queries.shape, queries.dtype)
+    whole = pl.BlockSpec(memory_space=pltpu.VMEM)
     return pl.pallas_call(
         functools.partial(kernel, tiles),
-        out_shape=(shape, shape),
+        out_shape=(kept, kept),
         in_specs=[anywhere] * 6 + [scalars] * 2,
-        out_specs=(anywhere, anywhere),
+        out_specs=(whole, whole),
         scratch_shapes=[
             pltpu.VMEM((5, heads, rows, 4 * D), queries.dtype),
             pltpu.VMEM((heads, rows, 2 * D), queries.dtype),
-            pltpu.VMEM((2, heads, rows, D), queries.dtype),
         ]
-        + [per_head] * 10
-        + [pltpu.SemaphoreType.DMA((2, heads))],
+        + [per_head] * 2
+        + [per_piece] * 2
+        + [per_head] * 2
+        + [per_piece] * 4,
+
         compiler_params=pltpu.CompilerParams(
             collective_id=0, has_side_effects=True, vmem_limit_bytes=56 * 1024 * 1024
         ),

time: 137 us -> 134 us (0.978)
  local copies, waits for them, and re-layouts: 3.62 us -> 2.11 us
    unnamed x4 -> x2, local copies, waits for them, and re-layouts: 3.62 us -> 2.11 us
    pallas_call x1, Pallas kernels: 132 us -> 131 us  [per_device(): pl.pallas_call(functools.partial(kernel, tiles), out_shape=(kept, kept),...]
where the time goes in v2:
time: 134 us
  Pallas kernels  131 us (98%)
  local copies, waits for them, and re-layouts  2.11 us (2%)
    pallas_call x1, Pallas kernels, per_device(): pl.pallas_call(functools.partial(kernel, tiles), out_shape=(kept, kept),...  131 us

profile of v2, /device:TPU:1, one launch (start us, length us, event | category | flops | bytes accessed | tf_op | source)
XLA Modules:
  0.0 134.3 jit_solution(2250370297711704327)
XLA Ops:
  1.3 130.8 %shard_map.95 = (bf16[256,2560]{1,0:T(8,128)(2,1)S(1)}, bf16[256,2560]{1,0:T(8,128)(2,1)S(1)}) custom-call(bf16[256,2560]{1,0:T(8,128)(2,1)} %q_ref.1, bf16[256,2560]{1,0:T(8,128)(2,1)} %k_ref.1, bf16[256,2560]{1,0:T(8,128)(2,1)} %v_ref.1, bf16[256,2560]{1,0:T(8,128)(2,1)} %qt_ref.1, bf16[256,2560]{1,0:T(8,128)(2,1)} %kt_ref.1, bf16[256,2560]{1,0:T(8,128)(2,1)} %vt_ref.1, ...), custom_call_target="tpu_custom_call" | custom-call | flops 10066329600 | bytes 10485760 | tf_op jit(solution)/shard_map/pallas_call | solution.py:230
  132.1 1.1 copy.12
  133.2 1.1 copy.13
